TPU v7x, 32 devices: a whole 2x2x4 slice. The times are simulated.
32 devices in a mesh: band: 8 (over z, x), sub: 4 (over y, core).
Axes of the slice: x: 2, y: 2, z: 4, core: 2. Of those that a mesh axis runs over, the one named last changes fastest.
Arguments:
- atmos_flux: bfloat16 [32, 64, 512], P(None, 'band', 'sub'), may hold values from -6 to 6
- weight_tiles: bfloat16 [8, 4, 32, 384, 128], P('band', 'sub'), may hold values from -0.3125 to 0.3125
- source_row: int32 [8, 4, 32], P('band', 'sub'), may hold values from 0 to 7
- target_code: int32 [8, 4, 32], P('band', 'sub'), may hold values from 0 to 63
- live_count: int32 [8, 4], P('band', 'sub'), may hold values from 8 to 32, as said below
Outputs:
- ocean_flux: float32 [32, 32768], P(None, ('band', 'sub'))
Inputs may be any that keep to these rules, and one draw needn't show every extreme that they name: `live_count`: each device has between 8 and 32 live entries; some device has exactly 32.
All inputs are finite; a program needn't handle non-finite values.
Results may differ from a plain program's by a relative error of at most 0.0036.
Values may be sent and summed in bfloat16 or wider, within the bound.
A program may use at most 64 MiB of HBM per device.

v0:
```python
import jax
import jax.numpy as jnp
from jax import lax
from jax.sharding import PartitionSpec as P

OB_DEV = 8


def with_halo(x, sides, width):
    for axis, dim in sides:
        count, length = (lax.axis_size(axis), x.shape[dim])
        up = [(i, (i + 1) % count) for i in range(count - 1)]
        down = [(j, i) for i, j in up]
        last = lax.slice_in_dim(x, length - width, length, axis=dim)
        leading = lax.slice_in_dim(x, 0, width, axis=dim)
        before = lax.ppermute(last, axis, up)
        after = lax.ppermute(leading, axis, down)
        x = jnp.concatenate([before, x, after], axis=dim)
    return x


def passed_along(value, axis, steps):
    count = lax.axis_size(axis)
    pairs = [(source, (source + steps) % count) for source in range(count)]
    return lax.ppermute(value, axis, pairs)


def shards(atmos_flux, weight_tiles, source_row, target_code, live_count):
    fields = atmos_flux.shape[0]
    width = atmos_flux.shape[2]
    capacity = weight_tiles.shape[2]
    subs = lax.axis_size("sub")
    owned = OB_DEV
    widened = with_halo(atmos_flux, (("band", 1), ("sub", 2)), 1)
    wide_float = widened.astype(jnp.float32)
    grad_x = (0.5 * (wide_float[:, 1:-1, 2:] - wide_float[:, 1:-1, :-2])).astype(jnp.bfloat16)
    grad_y = (0.5 * (wide_float[:, 2:, 1:-1] - wide_float[:, :-2, 1:-1])).astype(jnp.bfloat16)
    operand = jnp.concatenate([atmos_flux, grad_x, grad_y], axis=-1).transpose(1, 0, 2)
    picked = operand[source_row[0, 0]]
    product = jnp.einsum(
        "ekc,ecl->ekl", picked, weight_tiles[0, 0], preferred_element_type=jnp.float32
    )
    targets = 2 * subs * owned
    live = (jnp.arange(capacity, dtype=jnp.int32) < live_count[0, 0]).astype(jnp.float32)
    selector = (target_code[0, 0][None, :] == jnp.arange(targets, dtype=jnp.int32)[:, None]).astype(
        jnp.float32
    ) * live[None, :]
    summed = jnp.einsum("te,ekl->tkl", selector, product, precision=lax.Precision.HIGHEST)
    outgoing = summed.astype(jnp.bfloat16).reshape(subs, 2, owned, fields, width)
    received = lax.all_to_all(outgoing, "sub", split_axis=0, concat_axis=0, tiled=True)
    own_band = jnp.sum(received[:, 0].astype(jnp.float32), axis=0)
    arrived = passed_along(received[:, 1], "band", 1)
    next_band = jnp.sum(arrived.astype(jnp.float32), axis=0)
    total = own_band + next_band
    return total.transpose(1, 0, 2).reshape(fields, owned * width)


def solution(mesh):
    return jax.shard_map(
        shards,
        mesh=mesh,
        in_specs=(
            P(None, "band", "sub"),
            P("band", "sub", None, None, None),
            P("band", "sub", None),
            P("band", "sub", None),
            P("band", "sub"),
        ),
        out_specs=P(None, ("band", "sub")),
        check_vma=False,
    )
```

profile of v0, /device:TPU:0, one launch (start us, length us, event | category | flops | bytes accessed | tf_op | source)
XLA Modules:
  0.0 47.0 jit_solution(12757385105927854969)
XLA Ops:
  0.0 0.0 copy-start
  0.0 1.0 %copy.13 = bf16[32,8,128]{2,0,1:T(8,128)(2,1)S(1)} copy(bf16[32,8,128]{2,1,0:T(8,128)(2,1)} %param.5) | data formatting | bytes 131072 | tf_op args[0]
  1.0 4.8 %collective-permute-start = (bf16[32,1,128]{2,0,1:T(8,128)(2,1)S(1)}, bf16[32,1,128]{2,0,1:T(8,128)(2,1)S(1)}, u32[]{:S(2)}, u32[]{:S(2)}) collective-permute-start(bf16[32,1,128]{2,0,1:T(8,128)(2,1)S(1)} %get-tuple-element.10), channel_id=1, source_target_pairs={{0,4},{4,8},{8,12},{12,16},{16,20},{20,24},{24,28},{1,5},{5,9},{9,... | collective-permute-start | bytes 24584 | tf_op jit(solution)/shard_map/ppermute | solution.py:16
  5.9 1.3 %collective-permute-start.1 = (bf16[32,1,128]{2,0,1:T(8,128)(2,1)S(1)}, bf16[32,1,128]{2,0,1:T(8,128)(2,1)S(1)}, u32[]{:S(2)}, u32[]{:S(2)}) collective-permute-start(bf16[32,1,128]{2,0,1:T(8,128)(2,1)S(1)} %get-tuple-element.9), channel_id=1, source_target_pairs={{4,0},{8,4},{12,8},{16,12},{20,16},{24,20},{28,24},{5,1},{9,5},{13... | collective-permute-start | bytes 24584 | tf_op jit(solution)/shard_map/ppermute | solution.py:17
  7.2 0.7 %fusion.12 = s32[32]{0:T(128)S(1)} fusion(s32[1,1,32]{2,1,0:T(1,128)} %param.7), kind=kLoop, calls=%fused_computation.29 | loop fusion | flops 96 | bytes 256 | tf_op jit(solution)/shard_map/select_n | solution.py:39
  8.5 0.0 collective-permute-done
  8.5 0.9 %constant_dynamic-update-slice_fusion.1 = bf16[32,10,128]{2,0,1:T(8,128)(2,1)S(1)} fusion(bf16[32,10,128]{2,0,1:T(8,128)(2,1)S(1)} %constant_dynamic-update-slice_fusion.2, bf16[32,8,128]{2,1,0:T(8,128)(2,1)} %param.5), kind=kLoop, calls=%fused_computation.24 | loop fusion | bytes 131072
  9.4 2.0 %collective-permute-done.1 = bf16[32,1,128]{2,0,1:T(8,128)(2,1)S(1)} collective-permute-done((bf16[32,1,128]{2,0,1:T(8,128)(2,1)S(1)}, bf16[32,1,128]{2,0,1:T(8,128)(2,1)S(1)}, u32[]{:S(2)}, u32[]{:S(2)}) %collective-permute-start.1) | collective-permute-done | bytes 8224 | tf_op jit(solution)/shard_map/ppermute | solution.py:17
  11.4 0.1 fusion.14
  11.5 1.3 %collective-permute-start.2 = (bf16[32,10,1]{2,0,1:T(8,128)(2,1)S(1)}, bf16[32,10,1]{2,0,1:T(8,128)(2,1)S(1)}, u32[]{:S(2)}, u32[]{:S(2)}) collective-permute-start(bf16[32,10,1]{2,0,1:T(8,128)(2,1)S(1)} %get-tuple-element.7), channel_id=1, source_target_pairs={{0,1},{1,2},{2,3},{4,5},{5,6},{6,7},{8,9},{9,10},{10,11},{12,13},{... | collective-permute-start | bytes 1928 | tf_op jit(solution)/shard_map/ppermute | solution.py:16
  12.8 1.3 %collective-permute-start.3 = (bf16[32,10,1]{2,0,1:T(8,128)(2,1)S(1)}, bf16[32,10,1]{2,0,1:T(8,128)(2,1)S(1)}, u32[]{:S(2)}, u32[]{:S(2)}) collective-permute-start(bf16[32,10,1]{2,0,1:T(8,128)(2,1)S(1)} %get-tuple-element.8), channel_id=1, source_target_pairs={{1,0},{2,1},{3,2},{5,4},{6,5},{7,6},{9,8},{10,9},{11,10},{13,12},{... | collective-permute-start | bytes 1928 | tf_op jit(solution)/shard_map/ppermute | solution.py:17
  14.1 0.0 collective-permute-done.2
  14.1 3.6 %collective-permute-done.3 = bf16[32,10,1]{2,0,1:T(8,128)(2,1)S(1)} collective-permute-done((bf16[32,10,1]{2,0,1:T(8,128)(2,1)S(1)}, bf16[32,10,1]{2,0,1:T(8,128)(2,1)S(1)}, u32[]{:S(2)}, u32[]{:S(2)}) %collective-permute-start.3) | collective-permute-done | bytes 672 | tf_op jit(solution)/shard_map/ppermute | solution.py:17
  17.7 0.1 maximum_convert_fusion
  17.9 0.2 fusion.6
  18.1 0.0 copy-start.1
  18.1 1.5 %gather_fusion = bf16[32,32,384]{2,1,0:T(8,128)(2,1)} fusion(bf16[8,32,384]{2,1,0:T(8,128)(2,1)S(1)} %maximum_bitcast_fusion, s32[1024]{0:T(1024)S(1)} %pad_clamp_fusion), kind=kCustom, calls=%fused_computation | custom fusion | bytes 1572992 | tf_op jit(solution)/shard_map/gather | solution.py:39
  19.7 0.0 copy-done
  19.7 1.8 %fusion = f32[32,32,128]{2,1,0:T(8,128)S(1)} fusion(bf16[32,32,384]{2,1,0:T(8,128)(2,1)} %gather_fusion, bf16[1,1,32,384,128]{4,3,2,1,0:T(8,128)(2,1)S(1)} %copy-done), kind=kOutput, calls=%fused_computation.1 | convolution fusion | flops 100663296 | bytes 4456448 | tf_op jit(solution)/shard_map/ekc,ecl->ekl/dot_general | solution.py:40
  21.5 0.0 copy-done.1
  21.5 1.3 %convolution_convert_fusion = bf16[64,32,128]{2,0,1:T(8,128)(2,1)S(1)} fusion(f32[32,32,128]{2,1,0:T(8,128)S(1)} %fusion, f32[32]{0:T(128)S(1)} %compare_convert_fusion, s32[32]{0:T(128)S(1)} %bitcast.26), kind=kOutput, calls=%fused_computation.3 | convolution fusion | flops 100929536 | bytes 1048832 | tf_op jit(solution)/shard_map/te,ekl->tkl/dot_general | solution.py:48
  22.8 13.0 %all_to_all.5 = bf16[4,2,8,32,128]{4,2,1,3,0:T(8,128)(2,1)S(1)} all-to-all(bf16[4,2,8,32,128]{4,2,1,3,0:T(8,128)(2,1)S(1)} %copy.15), channel_id=1, replica_groups=mesh['band'=8,'sub'=4] {'sub'}, dimensions={0} | all-to-all | bytes 1048576 | tf_op jit(solution)/shard_map/all_to_all | solution.py:50
  35.9 2.5 %collective-permute-start.4 = (bf16[4,8,32,128]{3,1,2,0:T(8,128)(2,1)S(1)}, bf16[4,8,32,128]{3,1,2,0:T(8,128)(2,1)S(1)}, u32[]{:S(2)}, u32[]{:S(2)}) collective-permute-start(bf16[4,8,32,128]{3,1,2,0:T(8,128)(2,1)S(1)} %slice_bitcast_fusion), channel_id=1, source_target_pairs={{0,4},{4,8},{8,12},{12,16},{16,20},{20,24},{24,28},{28,0},{1,5},{5... | collective-permute-start | bytes 786440 | tf_op jit(solution)/shard_map/ppermute | solution.py:25
  38.4 7.9 %collective-permute-done.4 = bf16[4,8,32,128]{3,1,2,0:T(8,128)(2,1)S(1)} collective-permute-done((bf16[4,8,32,128]{3,1,2,0:T(8,128)(2,1)S(1)}, bf16[4,8,32,128]{3,1,2,0:T(8,128)(2,1)S(1)}, u32[]{:S(2)}, u32[]{:S(2)}) %collective-permute-start.4) | collective-permute-done | bytes 262176 | tf_op jit(solution)/shard_map/ppermute | solution.py:25
  46.4 0.7 %copy.21 = f32[4,8,8,128]{3,1,2,0:T(8,128)} copy(f32[4,8,8,128]{3,2,1,0:T(8,128)S(1)} %bitcast.25) | data formatting | bytes 262144
  (11 shorter events, 0.2 us)
Async XLA Ops:
  0.0 19.7 %copy-start = (bf16[1,1,32,384,128]{4,3,2,1,0:T(8,128)(2,1)S(1)}, bf16[1,1,32,384,128]{4,3,2,1,0:T(8,128)(2,1)}, u32[]{:S(2)}) copy-start(bf16[1,1,32,384,128]{4,3,2,1,0:T(8,128)(2,1)} %param.6) | copy-start | bytes 9437188
  1.0 7.5 %collective-permute-start = (bf16[32,1,128]{2,0,1:T(8,128)(2,1)S(1)}, bf16[32,1,128]{2,0,1:T(8,128)(2,1)S(1)}, u32[]{:S(2)}, u32[]{:S(2)}) collective-permute-start(bf16[32,1,128]{2,0,1:T(8,128)(2,1)S(1)} %get-tuple-element.10), channel_id=1, source_target_pairs={{0,4},{4,8},{8,12},{12,16},{16,20},{20,24},{24,28},{1,5},{5,9},{9,... | collective-permute-start | bytes 24584 | tf_op jit(solution)/shard_map/ppermute | solution.py:16
  5.9 5.5 %collective-permute-start.1 = (bf16[32,1,128]{2,0,1:T(8,128)(2,1)S(1)}, bf16[32,1,128]{2,0,1:T(8,128)(2,1)S(1)}, u32[]{:S(2)}, u32[]{:S(2)}) collective-permute-start(bf16[32,1,128]{2,0,1:T(8,128)(2,1)S(1)} %get-tuple-element.9), channel_id=1, source_target_pairs={{4,0},{8,4},{12,8},{16,12},{20,16},{24,20},{28,24},{5,1},{9,5},{13... | collective-permute-start | bytes 24584 | tf_op jit(solution)/shard_map/ppermute | solution.py:17
  11.5 2.6 %collective-permute-start.2 = (bf16[32,10,1]{2,0,1:T(8,128)(2,1)S(1)}, bf16[32,10,1]{2,0,1:T(8,128)(2,1)S(1)}, u32[]{:S(2)}, u32[]{:S(2)}) collective-permute-start(bf16[32,10,1]{2,0,1:T(8,128)(2,1)S(1)} %get-tuple-element.7), channel_id=1, source_target_pairs={{0,1},{1,2},{2,3},{4,5},{5,6},{6,7},{8,9},{9,10},{10,11},{12,13},{... | collective-permute-start | bytes 1928 | tf_op jit(solution)/shard_map/ppermute | solution.py:16
  12.8 4.9 %collective-permute-start.3 = (bf16[32,10,1]{2,0,1:T(8,128)(2,1)S(1)}, bf16[32,10,1]{2,0,1:T(8,128)(2,1)S(1)}, u32[]{:S(2)}, u32[]{:S(2)}) collective-permute-start(bf16[32,10,1]{2,0,1:T(8,128)(2,1)S(1)} %get-tuple-element.8), channel_id=1, source_target_pairs={{1,0},{2,1},{3,2},{5,4},{6,5},{7,6},{9,8},{10,9},{11,10},{13,12},{... | collective-permute-start | bytes 1928 | tf_op jit(solution)/shard_map/ppermute | solution.py:17
  18.1 3.4 %copy-start.1 = (s32[1,1,32]{2,1,0:T(1,128)S(1)}, s32[1,1,32]{2,1,0:T(1,128)}, u32[]{:S(2)}) copy-start(s32[1,1,32]{2,1,0:T(1,128)} %param.8) | copy-start | bytes 388
  35.9 10.4 %collective-permute-start.4 = (bf16[4,8,32,128]{3,1,2,0:T(8,128)(2,1)S(1)}, bf16[4,8,32,128]{3,1,2,0:T(8,128)(2,1)S(1)}, u32[]{:S(2)}, u32[]{:S(2)}) collective-permute-start(bf16[4,8,32,128]{3,1,2,0:T(8,128)(2,1)S(1)} %slice_bitcast_fusion), channel_id=1, source_target_pairs={{0,4},{4,8},{8,12},{12,16},{16,20},{20,24},{24,28},{28,0},{1,5},{5... | collective-permute-start | bytes 786440 | tf_op jit(solution)/shard_map/ppermute | solution.py:25
where the time goes:
time: 47.4 us; the launch traced here: 47 us
  waiting for transfers between devices  13.5 us (28%)
  blocking collectives  13 us (27%)
  starting transfers between devices  11.2 us (24%)
  local copies, waits for them, and re-layouts  4.29 us (9%)
  matrix products  3.08 us (6%)
  other arithmetic  1.09 us (2%)
  between operations  0.81 us (2%)
    all_to_all x1, blocking collectives, shards(): lax.all_to_all(outgoing, 'sub', split_axis=0, concat_axis=0, tiled=True)  13 us
    ppermute x1, waiting for transfers between devices, passed_along(): return lax.ppermute(value, axis, pairs)  7.89 us
    ppermute x2, starting transfers between devices, with_halo(): before = lax.ppermute(last, axis, up)  6.14 us
    ppermute x2, waiting for transfers between devices, with_halo(): after = lax.ppermute(leading, axis, down)  5.64 us
    ppermute x2, starting transfers between devices, with_halo(): after = lax.ppermute(leading, axis, down)  2.58 us
    unnamed x8, local copies, waits for them, and re-layouts  2.56 us
    ppermute x1, starting transfers between devices, passed_along(): return lax.ppermute(value, axis, pairs)  2.5 us
    dot_general x1, matrix products, shards(): jnp.einsum('ekc,ecl->ekl', picked, weight_tiles[0, 0], preferred_element_...  1.79 us
  transfers between devices with their start and end apart: 5, of which 3 were waited for; matrix products, arithmetic and copies ran while one was open for 3% of the time, Pallas kernels for 0%

commit v1 on v0

v1 whole, which is shorter than its diff:
```python
import functools

import jax
import jax.numpy as jnp
from jax import lax
from jax.experimental import pallas as pl
from jax.experimental.pallas import tpu as pltpu
from jax.sharding import PartitionSpec as P

OB_DEV = 8
MESH = pl.DeviceIdType.MESH


def kernel(
    sizes, idx_ref, flux_ref, weight_ref, out_ref,
    xin, x32, op, wv, prefix, halo_out, halo_in, a_out, a_in, b_out, b_in,
    in_sem, halo_send, halo_recv, a_send, a_recv, b_send, b_recv,
):
    fields, rows, width, cap, bands, subs = sizes
    ny = subs // 2
    b = lax.axis_index("band")
    s = lax.axis_index("sub")
    y, core = s // 2, s % 2
    up, down = (b + 1) % bands, (b + bands - 1) % bands

    copy_flux = pltpu.make_async_copy(flux_ref, xin, in_sem.at[0])
    copy_flux.start()
    copy_w0 = pltpu.make_async_copy(weight_ref.at[:, :width], wv.at[:, :width], in_sem.at[1])
    copy_w0.start()
    half = cap // 2
    copy_w = []
    for part in range(2):
        where = (pl.ds(part * half, half), pl.ds(width, 2 * width))
        copy_w.append(pltpu.make_async_copy(weight_ref.at[where], wv.at[where], in_sem.at[2 + part]))
        copy_w[-1].start()

    barrier = pltpu.get_barrier_semaphore()
    for other in range(1, subs):
        pl.semaphore_signal(barrier, inc=1, device_id=(b, (s + other) % subs), device_id_type=MESH)
    for other in range(ny):
        pl.semaphore_signal(barrier, inc=1, device_id=(up, other * 2 + core), device_id_type=MESH)
        pl.semaphore_signal(barrier, inc=1, device_id=(down, other * 2 + core), device_id_type=MESH)

    copy_flux.wait()
    x32[...] = xin[...].astype(jnp.float32)
    lane = lax.broadcasted_iota(jnp.int32, (fields, width), 1)

    def row(i):
        return x32[pl.ds(i, fields, stride=rows), :]

    first = jnp.zeros((fields, width), jnp.float32)
    last = jnp.zeros((fields, width), jnp.float32)
    for i in range(rows):
        x = row(i)
        op[i, :, :width] = x.astype(jnp.bfloat16)
        first = jnp.where(lane == i, x[:, :1], first)
        last = jnp.where(lane == i, x[:, width - 1:], last)
    halo_out[0] = row(rows - 1).astype(jnp.bfloat16)
    halo_out[1] = row(0).astype(jnp.bfloat16)
    halo_out[2] = last.astype(jnp.bfloat16)
    halo_out[3] = first.astype(jnp.bfloat16)
    prefix[cap] = jnp.zeros((fields, width), jnp.float32)

    pl.semaphore_wait(barrier, subs - 1 + 2 * ny)

    partners = ((up, s), (down, s), (b, (s + 1) % subs), (b, (s + subs - 1) % subs))
    sends = (b < bands - 1, b > 0, s < subs - 1, s > 0)
    receives = (b > 0, b < bands - 1, s > 0, s < subs - 1)
    halos = [
        pltpu.make_async_remote_copy(
            src_ref=halo_out.at[k], dst_ref=halo_in.at[k], send_sem=halo_send.at[k], recv_sem=halo_recv.at[k],
            device_id=partners[k], device_id_type=MESH)
        for k in range(4)
    ]
    for k in range(4):
        @pl.when(sends[k])
        def _(k=k):
            halos[k].start()

    copy_w0.wait()

    def flux_part(e, carry):
        picked = op[idx_ref[e], :, :width]
        prefix[e] = jnp.dot(picked, wv[e, :width], preferred_element_type=jnp.float32)
        return carry

    lax.fori_loop(0, cap, flux_part, 0, unroll=True)

    for k in range(4):
        @pl.when(receives[k])
        def _(k=k):
            halos[k].wait_recv()

        @pl.when(jnp.logical_not(receives[k]))
        def _(k=k):
            halo_in[k] = jnp.zeros((fields, width), jnp.bfloat16)

    below, above, left, right = (halo_in[k].astype(jnp.float32) for k in range(4))
    for i in range(rows):
        x = row(i)
        before = row(i - 1) if i > 0 else below
        after = row(i + 1) if i < rows - 1 else above
        west = jnp.where(lane == 0, left[:, i:i + 1], pltpu.roll(x, 1, 1))
        east = jnp.where(lane == width - 1, right[:, i:i + 1], pltpu.roll(x, width - 1, 1))
        op[i, :, width:2 * width] = (0.5 * (east - west)).astype(jnp.bfloat16)
        op[i, :, 2 * width:] = (0.5 * (after - before)).astype(jnp.bfloat16)

    def gradient_part(e, carry):
        picked = op[idx_ref[e], :, width:]
        product = jnp.dot(picked, wv[e, width:], preferred_element_type=jnp.float32)
        prefix[e] = prefix[e] + product + prefix[idx_ref[cap + e]]
        return carry

    for part in range(2):
        copy_w[part].wait()
        lax.fori_loop(part * half, (part + 1) * half, gradient_part, 0, unroll=True)

    def partial(sub, step, q):
        return prefix[idx_ref[2 * cap + (sub * 2 + step) * OB_DEV + q]]

    pieces = [(j, 1) for j in range(1, ny)] + [(0, 1)] + [(j, 0) for j in range(1, ny)] + [(0, 0)]
    swaps, moves = [], []
    for p, (j, step) in enumerate(pieces):
        target = (y + j) % ny * 2 + 1 - core
        for q in range(OB_DEV):
            a_out[p, q] = partial(target, step, q).astype(jnp.bfloat16)
        swaps.append(pltpu.make_async_remote_copy(
            src_ref=a_out.at[p], dst_ref=a_in.at[p], send_sem=a_send.at[p], recv_sem=a_recv.at[p],
            device_id=(b, y * 2 + 1 - core), device_id_type=MESH))
        swaps[-1].start()
    for p, (j, step) in enumerate(pieces):
        target = (y + j) % ny * 2 + core
        swaps[p].wait_recv()
        if (j, step) == (0, 0):
            for q in range(OB_DEV):
                out_ref[:, q * width:(q + 1) * width] = partial(target, step, q) + a_in[p, q].astype(jnp.float32)
            continue
        for q in range(OB_DEV):
            b_out[p, q] = (partial(target, step, q) + a_in[p, q].astype(jnp.float32)).astype(jnp.bfloat16)
        moves.append(pltpu.make_async_remote_copy(
            src_ref=b_out.at[p], dst_ref=b_in.at[p], send_sem=b_send.at[p], recv_sem=b_recv.at[p],
            device_id=(up if step else b, target), device_id_type=MESH))
        moves[-1].start()
    for move in moves:
        move.wait_recv()
    for q in range(OB_DEV):
        total = out_ref[:, q * width:(q + 1) * width]
        for p in range(len(moves)):
            total = total + b_in[p, q].astype(jnp.float32)
        out_ref[:, q * width:(q + 1) * width] = total

    for k in range(4):
        @pl.when(sends[k])
        def _(k=k):
            halos[k].wait_send()
    for copy in swaps + moves:
        copy.wait_send()


def shards(atmos_flux, weight_tiles, source_row, target_code, live_count):
    fields, rows, width = atmos_flux.shape
    cap = weight_tiles.shape[2]
    bands, subs = lax.axis_size("band"), lax.axis_size("sub")
    targets = 2 * subs * OB_DEV
    pieces = subs

    code = target_code[0, 0]
    entry = jnp.arange(cap, dtype=jnp.int32)
    wanted = jnp.concatenate([code, jnp.arange(targets, dtype=jnp.int32)])
    limit = jnp.concatenate([entry, jnp.full((targets,), live_count[0, 0], jnp.int32)])
    match = (wanted[:, None] == code[None, :]) & (entry[None, :] < limit[:, None])
    found = jnp.max(jnp.where(match, entry[None, :], -1), axis=1)
    found = jnp.where(found < 0, cap, found)
    table = jnp.concatenate([source_row[0, 0], found])

    block = (OB_DEV, fields, width)
    return pl.pallas_call(
        functools.partial(kernel, (fields, rows, width, cap, bands, subs)),
        out_shape=jax.ShapeDtypeStruct((fields, OB_DEV * width), jnp.float32),
        in_specs=[
            pl.BlockSpec(memory_space=pltpu.SMEM),
            pl.BlockSpec(memory_space=pltpu.HBM),
            pl.BlockSpec(memory_space=pltpu.HBM),
        ],
        out_specs=pl.BlockSpec(memory_space=pltpu.VMEM),
        scratch_shapes=[
            pltpu.VMEM((fields * rows, width), jnp.bfloat16),
            pltpu.VMEM((fields * rows, width), jnp.float32),
            pltpu.VMEM((rows, fields, 3 * width), jnp.bfloat16),
            pltpu.VMEM((cap, 3 * width, width), jnp.bfloat16),
            pltpu.VMEM((cap + 1, fields, width), jnp.float32),
            pltpu.VMEM((4, fields, width), jnp.bfloat16),
            pltpu.VMEM((4, fields, width), jnp.bfloat16),
            pltpu.VMEM((pieces,) + block, jnp.bfloat16),
            pltpu.VMEM((pieces,) + block, jnp.bfloat16),
            pltpu.VMEM((pieces - 1,) + block, jnp.bfloat16),
            pltpu.VMEM((pieces - 1,) + block, jnp.bfloat16),
            pltpu.SemaphoreType.DMA((4,)),
            pltpu.SemaphoreType.DMA((4,)),
            pltpu.SemaphoreType.DMA((4,)),
            pltpu.SemaphoreType.DMA((pieces,)),
            pltpu.SemaphoreType.DMA((pieces,)),
            pltpu.SemaphoreType.DMA((pieces - 1,)),
            pltpu.SemaphoreType.DMA((pieces - 1,)),
        ],
        compiler_params=pltpu.CompilerParams(
            collective_id=0, has_side_effects=True, vmem_limit_bytes=24 * 1024 * 1024
        ),
    )(table, atmos_flux.reshape(fields * rows, width), weight_tiles[0, 0])


def solution(mesh):
    return jax.shard_map(
        shards,
        mesh=mesh,
        in_specs=(
            P(None, "band", "sub"),
            P("band", "sub", None, None, None),
            P("band", "sub", None),
            P("band", "sub", None),
            P("band", "sub"),
        ),
        out_specs=P(None, ("band", "sub")),
        check_vma=False,
    )
```

time: 47.4 us -> 23.1 us (0.49)
  Pallas kernels: 0 us -> 16.6 us
  waiting for transfers between devices: 13.5 us -> 0 us
  blocking collectives: 13 us -> 0 us
  starting transfers between devices: 11.2 us -> 0 us
  matrix products: 3.08 us -> 0 us
  other arithmetic: 1.09 us -> 2.22 us
  local copies, waits for them, and re-layouts: 4.29 us -> 3.4 us
    pallas_call x0 -> x1, Pallas kernels: none -> 16.6 us  [shards(): pl.pallas_call(functools.partial(kernel, (fields, rows, width, cap, bands...]
    ppermute x5 -> x0, waiting for transfers between devices: 13.5 us -> none  [the longest x1 7.89 us: passed_along(): return lax.ppermute(value, axis, pairs)]
    all_to_all x1 -> x0, blocking collectives: 13 us -> none  [shards(): lax.all_to_all(outgoing, 'sub', split_axis=0, concat_axis=0, tiled=True)]
    ppermute x5 -> x0, starting transfers between devices: 11.2 us -> none  [the longest x2 6.14 us: with_halo(): before = lax.ppermute(last, axis, up)]
    dot_general x2 -> x0, matrix products: 3.08 us -> none  [the longest x1 1.79 us: shards(): jnp.einsum('ekc,ecl->ekl', picked, weight_tiles[0, 0], preferred_element_...]
    gather x1 -> x0, local copies, waits for them, and re-layouts: 1.54 us -> none  [shards(): picked = operand[source_row[0, 0]]]
    concatenate x0 -> x2, other arithmetic: none -> 1.47 us  [the longest x1 0.73 us: shards(): wanted = jnp.concatenate([code, jnp.arange(targets, dtype=jnp.int32)])]
    unnamed x8 -> x5, local copies, waits for them, and re-layouts: 2.56 us -> 3.39 us
  transfers between devices with their start and end apart: 5 -> 0, of which waited for: 3 -> 0; matrix products, arithmetic and copies ran while one was open for 3% -> 0% of each run, Pallas kernels for 0% -> 0%
where the time goes in v1:
time: 23.1 us; the launch traced here: 22.9 us
  Pallas kernels  16.6 us (72%)
  local copies, waits for them, and re-layouts  3.4 us (15%)
  other arithmetic  2.22 us (10%)
  between operations  0.69 us (3%)
    pallas_call x1, Pallas kernels, shards(): pl.pallas_call(functools.partial(kernel, (fields, rows, width, cap, bands...  16.6 us
    unnamed x5, local copies, waits for them, and re-layouts  3.39 us
    reduce_max x1, other arithmetic, shards(): found = jnp.max(jnp.where(match, entry[None, :], -1), axis=1)  0.74 us
    concatenate x1, other arithmetic, shards(): wanted = jnp.concatenate([code, jnp.arange(targets, dtype=jnp.int32)])  0.73 us
    concatenate x1, other arithmetic, shards(): table = jnp.concatenate([source_row[0, 0], found])  0.73 us

profile of v1, /device:TPU:0, one launch (start us, length us, event | category | flops | bytes accessed | tf_op | source)
XLA Modules:
  0.0 22.9 jit_solution(4082554565607472951)
XLA Ops:
  0.7 0.7 %pad_add_fusion = s32[96]{0:T(128)S(1)} fusion(s32[64]{0:T(128)S(1)} %iota.9, s32[32]{0:T(128)} %bitcast.8), kind=kLoop, calls=%fused_computation.4 | loop fusion | flops 96 | bytes 768 | tf_op jit(solution)/shard_map/concatenate | solution.py:169
  1.4 0.7 %select_reduce_fusion = s32[96]{0:T(128)S(1)} fusion(s32[96]{0:T(128)S(1)} %concatenate.10, s32[96]{0:T(128)S(1)} %pad_add_fusion, s32[32]{0:T(128)} %bitcast.9), kind=kLoop, calls=%fused_computation | loop fusion | flops 15264 | bytes 1280 | tf_op jit(solution)/shard_map/reduce_max | solution.py:172
  2.2 0.7 %pad_add_fusion.1.idx_ref = s32[128]{0:T(128)S(1)} fusion(s32[96]{0:T(128)S(1)} %compare_select_fusion, s32[32]{0:T(128)} %bitcast.10), kind=kLoop, calls=%fused_computation.5 | loop fusion | flops 128 | bytes 1024 | tf_op jit(solution)/shard_map/concatenate | solution.py:174
  2.9 0.0 copy-start
  2.9 1.9 %copy-done = bf16[1,1,32,384,128]{4,3,2,1,0:T(8,128)(2,1)S(1)} copy-done((bf16[1,1,32,384,128]{4,3,2,1,0:T(8,128)(2,1)S(1)}, bf16[1,1,32,384,128]{4,3,2,1,0:T(8,128)(2,1)}, u32[]{:S(2)}) %copy-start) | copy-done | bytes 3145752
  4.8 0.0 copy-start.1
  4.8 0.8 %copy-done.1 = bf16[32,8,128]{2,1,0:T(8,128)(2,1)S(1)} copy-done((bf16[32,8,128]{2,1,0:T(8,128)(2,1)S(1)}, bf16[32,8,128]{2,1,0:T(8,128)(2,1)}, u32[]{:S(2)}) %copy-start.1) | copy-done | bytes 65560
  5.6 16.6 %shard_map.55 = f32[32,1024]{1,0:T(8,128)S(1)} custom-call(s32[128]{0:T(128)S(1)} %pad_add_fusion.1.idx_ref, bf16[256,128]{1,0:T(8,128)(2,1)S(1)} %bitcast.7, bf16[32,384,128]{2,1,0:T(8,128)(2,1)S(1)} %bitcast.6), custom_call_target="tpu_custom_call" | custom-call | tf_op jit(solution)/shard_map/pallas_call | solution.py:177
  22.2 0.7 %copy.8 = f32[32,1024]{1,0:T(8,128)} copy(f32[32,1024]{1,0:T(8,128)S(1)} %shard_map.55) | data formatting | bytes 262144
  (4 shorter events, 0.0 us)
Async XLA Ops:
  2.9 1.9 %copy-start = (bf16[1,1,32,384,128]{4,3,2,1,0:T(8,128)(2,1)S(1)}, bf16[1,1,32,384,128]{4,3,2,1,0:T(8,128)(2,1)}, u32[]{:S(2)}) copy-start(bf16[1,1,32,384,128]{4,3,2,1,0:T(8,128)(2,1)} %param.6) | copy-start | bytes 9437188
  4.8 0.8 %copy-start.1 = (bf16[32,8,128]{2,1,0:T(8,128)(2,1)S(1)}, bf16[32,8,128]{2,1,0:T(8,128)(2,1)}, u32[]{:S(2)}) copy-start(bf16[32,8,128]{2,1,0:T(8,128)(2,1)} %param.5) | copy-start | bytes 196612

commit v2 on v1

--- a/solution.py
+++ b/solution.py
@@ -12,8 +12,8 @@
 
 
 def kernel(
-    sizes, idx_ref, flux_ref, weight_ref, out_ref,
-    xin, x32, op, wv, prefix, halo_out, halo_in, a_out, a_in, b_out, b_in,
+    sizes, row_ref, code_ref, live_ref, flux_ref, weight_ref, out_ref,
+    table, found, xin, x32, op, wv, prefix, halo_out, halo_in, a_out, a_in, b_out, b_in,
     in_sem, halo_send, halo_recv, a_send, a_recv, b_send, b_recv,
 ):
     fields, rows, width, cap, bands, subs = sizes
@@ -40,6 +40,19 @@
     for other in range(ny):
         pl.semaphore_signal(barrier, inc=1, device_id=(up, other * 2 + core), device_id_type=MESH)
         pl.semaphore_signal(barrier, inc=1, device_id=(down, other * 2 + core), device_id_type=MESH)
+
+    part_row = lax.broadcasted_iota(jnp.int32, table.shape, 0)
+    part_lane = lax.broadcasted_iota(jnp.int32, table.shape, 1)
+    wanted = (part_row - 1) * table.shape[1] + part_lane
+    for e in range(cap):
+        wanted = jnp.where((part_row == 0) & (part_lane == e), code_ref[e], wanted)
+    limit = jnp.where(part_row == 0, part_lane, live_ref[0, 0])
+    entry = jnp.full(table.shape, cap, jnp.int32)
+    for e in range(cap):
+        entry = jnp.where((wanted == code_ref[e]) & (limit > e), e, entry)
+    table[...] = entry
+    copy_found = pltpu.make_async_copy(table, found, in_sem.at[4])
+    copy_found.start()
 
     copy_flux.wait()
     x32[...] = xin[...].astype(jnp.float32)
@@ -80,7 +93,7 @@
     copy_w0.wait()
 
     def flux_part(e, carry):
-        picked = op[idx_ref[e], :, :width]
+        picked = op[row_ref[e], :, :width]
         prefix[e] = jnp.dot(picked, wv[e, :width], preferred_element_type=jnp.float32)
         return carry
 
@@ -106,17 +119,19 @@
         op[i, :, 2 * width:] = (0.5 * (after - before)).astype(jnp.bfloat16)
 
     def gradient_part(e, carry):
-        picked = op[idx_ref[e], :, width:]
+        picked = op[row_ref[e], :, width:]
         product = jnp.dot(picked, wv[e, width:], preferred_element_type=jnp.float32)
-        prefix[e] = prefix[e] + product + prefix[idx_ref[cap + e]]
+        prefix[e] = prefix[e] + product + prefix[found[0, e]]
         return carry
 
+    copy_found.wait()
     for part in range(2):
         copy_w[part].wait()
         lax.fori_loop(part * half, (part + 1) * half, gradient_part, 0, unroll=True)
 
     def partial(sub, step, q):
-        return prefix[idx_ref[2 * cap + (sub * 2 + step) * OB_DEV + q]]
+        t = (sub * 2 + step) * OB_DEV + q
+        return prefix[found[1 + t // found.shape[1], t % found.shape[1]]]
 
     pieces = [(j, 1) for j in range(1, ny)] + [(0, 1)] + [(j, 0) for j in range(1, ny)] + [(0, 0)]
     swaps, moves = [], []
@@ -164,26 +179,22 @@
     targets = 2 * subs * OB_DEV
     pieces = subs
 
-    code = target_code[0, 0]
-    entry = jnp.arange(cap, dtype=jnp.int32)
-    wanted = jnp.concatenate([code, jnp.arange(targets, dtype=jnp.int32)])
-    limit = jnp.concatenate([entry, jnp.full((targets,), live_count[0, 0], jnp.int32)])
-    match = (wanted[:, None] == code[None, :]) & (entry[None, :] < limit[:, None])
-    found = jnp.max(jnp.where(match, entry[None, :], -1), axis=1)
-    found = jnp.where(found < 0, cap, found)
-    table = jnp.concatenate([source_row[0, 0], found])
-
+    table = (-(-(1 + -(-targets // 128)) // 8) * 8, 128)
     block = (OB_DEV, fields, width)
     return pl.pallas_call(
         functools.partial(kernel, (fields, rows, width, cap, bands, subs)),
         out_shape=jax.ShapeDtypeStruct((fields, OB_DEV * width), jnp.float32),
         in_specs=[
             pl.BlockSpec(memory_space=pltpu.SMEM),
+            pl.BlockSpec(memory_space=pltpu.SMEM),
+            pl.BlockSpec(memory_space=pltpu.SMEM),
             pl.BlockSpec(memory_space=pltpu.HBM),
             pl.BlockSpec(memory_space=pltpu.HBM),
         ],
         out_specs=pl.BlockSpec(memory_space=pltpu.VMEM),
         scratch_shapes=[
+            pltpu.VMEM(table, jnp.int32),
+            pltpu.SMEM(table, jnp.int32),
             pltpu.VMEM((fields * rows, width), jnp.bfloat16),
             pltpu.VMEM((fields * rows, width), jnp.float32),
             pltpu.VMEM((rows, fields, 3 * width), jnp.bfloat16),
@@ -195,7 +206,7 @@
             pltpu.VMEM((pieces,) + block, jnp.bfloat16),
             pltpu.VMEM((pieces - 1,) + block, jnp.bfloat16),
             pltpu.VMEM((pieces - 1,) + block, jnp.bfloat16),
-            pltpu.SemaphoreType.DMA((4,)),
+            pltpu.SemaphoreType.DMA((5,)),
             pltpu.SemaphoreType.DMA((4,)),
             pltpu.SemaphoreType.DMA((4,)),
             pltpu.SemaphoreType.DMA((pieces,)),
@@ -204,9 +215,9 @@
             pltpu.SemaphoreType.DMA((pieces - 1,)),
         ],
         compiler_params=pltpu.CompilerParams(
-            collective_id=0, has_side_effects=True, vmem_limit_bytes=24 * 1024 * 1024
+            collective_id=0, has_side_effects=True, vmem_limit_bytes=60 * 1024 * 1024
         ),
-    )(table, atmos_flux.reshape(fields * rows, width), weight_tiles[0, 0])
+    )(source_row[0, 0], target_code[0, 0], live_count, atmos_flux.reshape(fields * rows, width), weight_tiles[0, 0])
 
 
 def solution(mesh):

time: 23.1 us -> 19.8 us (0.86)
  other arithmetic: 2.22 us -> 0 us
  local copies, waits for them, and re-layouts: 3.4 us -> 1.57 us
  Pallas kernels: 16.6 us -> 17.5 us
    unnamed x5 -> x1, local copies, waits for them, and re-layouts: 3.39 us -> 1.57 us
    concatenate x2 -> x0, other arithmetic: 1.47 us -> none  [the longest x1 0.73 us: shards(): wanted = jnp.concatenate([code, jnp.arange(targets, dtype=jnp.int32)])]
    pallas_call x1, Pallas kernels: 16.6 us -> 17.5 us  [shards(): pl.pallas_call(functools.partial(kernel, (fields, rows, width, cap, bands...]
    reduce_max x1 -> x0, other arithmetic: 0.74 us -> none  [shards(): found = jnp.max(jnp.where(match, entry[None, :], -1), axis=1)]
where the time goes in v2:
time: 19.8 us; the launch traced here: 19.7 us
  Pallas kernels  17.5 us (88%)
  local copies, waits for them, and re-layouts  1.57 us (8%)
  between operations  0.66 us (3%)
    pallas_call x1, Pallas kernels, shards(): pl.pallas_call(functools.partial(kernel, (fields, rows, width, cap, bands...  17.5 us
    unnamed x1, local copies, waits for them, and re-layouts  1.57 us

profile of v2, /device:TPU:0, one launch (start us, length us, event | category | flops | bytes accessed | tf_op | source)
XLA Modules:
  0.0 19.7 jit_solution(13006670661912700896)
XLA Ops:
  0.7 17.5 %shard_map.55 = f32[32,1024]{1,0:T(8,128)} custom-call(s32[32]{0:T(128)} %bitcast.6, s32[32]{0:T(128)} %bitcast.7, s32[1,1]{1,0:T(1,128)S(6)} %copy.7.live_ref, bf16[256,128]{1,0:T(8,128)(2,1)} %bitcast.5, bf16[32,384,128]{2,1,0:T(8,128)(2,1)} %bitcast.4), custom_call_target="tpu_custom_call" | custom-call | tf_op jit(solution)/shard_map/pallas_call | solution.py:184
  18.1 1.6 %copy.8 = f32[32,1024]{1,0:T(8,128)} copy(f32[32,1024]{1,0:T(8,128)} %shard_map.55) | data formatting | bytes 262144

commit v3 on v2

--- a/solution.py
+++ b/solution.py
@@ -43,7 +43,7 @@
 
     part_row = lax.broadcasted_iota(jnp.int32, table.shape, 0)
     part_lane = lax.broadcasted_iota(jnp.int32, table.shape, 1)
-    wanted = (part_row - 1) * table.shape[1] + part_lane
+    wanted = jnp.where(part_lane < 2 * OB_DEV, (part_row - 1) * 2 * OB_DEV + part_lane, -1)
     for e in range(cap):
         wanted = jnp.where((part_row == 0) & (part_lane == e), code_ref[e], wanted)
     limit = jnp.where(part_row == 0, part_lane, live_ref[0, 0])
@@ -121,17 +121,21 @@
     def gradient_part(e, carry):
         picked = op[row_ref[e], :, width:]
         product = jnp.dot(picked, wv[e, width:], preferred_element_type=jnp.float32)
-        prefix[e] = prefix[e] + product + prefix[found[0, e]]
+        prefix[e] = prefix[e] + product
         return carry
 
-    copy_found.wait()
+    def chain(e, carry):
+        prefix[e] = prefix[e] + prefix[found[0, e]]
+        return carry
+
     for part in range(2):
         copy_w[part].wait()
         lax.fori_loop(part * half, (part + 1) * half, gradient_part, 0, unroll=True)
+    copy_found.wait()
+    lax.fori_loop(0, cap, chain, 0, unroll=True)
 
     def partial(sub, step, q):
-        t = (sub * 2 + step) * OB_DEV + q
-        return prefix[found[1 + t // found.shape[1], t % found.shape[1]]]
+        return prefix[found[1 + sub, step * OB_DEV + q]]
 
     pieces = [(j, 1) for j in range(1, ny)] + [(0, 1)] + [(j, 0) for j in range(1, ny)] + [(0, 0)]
     swaps, moves = [], []
@@ -156,13 +160,10 @@
             src_ref=b_out.at[p], dst_ref=b_in.at[p], send_sem=b_send.at[p], recv_sem=b_recv.at[p],
             device_id=(up if step else b, target), device_id_type=MESH))
         moves[-1].start()
-    for move in moves:
+    for p, move in enumerate(moves):
         move.wait_recv()
-    for q in range(OB_DEV):
-        total = out_ref[:, q * width:(q + 1) * width]
-        for p in range(len(moves)):
-            total = total + b_in[p, q].astype(jnp.float32)
-        out_ref[:, q * width:(q + 1) * width] = total
+        for q in range(OB_DEV):
+            out_ref[:, q * width:(q + 1) * width] += b_in[p, q].astype(jnp.float32)
 
     for k in range(4):
         @pl.when(sends[k])
@@ -176,14 +177,13 @@
     fields, rows, width = atmos_flux.shape
     cap = weight_tiles.shape[2]
     bands, subs = lax.axis_size("band"), lax.axis_size("sub")
-    targets = 2 * subs * OB_DEV
     pieces = subs
 
-    table = (-(-(1 + -(-targets // 128)) // 8) * 8, 128)
+    table = (-(-(1 + subs) // 8) * 8, 128)
     block = (OB_DEV, fields, width)
     return pl.pallas_call(
         functools.partial(kernel, (fields, rows, width, cap, bands, subs)),
-        out_shape=jax.ShapeDtypeStruct((fields, OB_DEV * width), jnp.float32),
+        out_shape=pltpu.VMEM((fields, OB_DEV * width), jnp.float32),
         in_specs=[
             pl.BlockSpec(memory_space=pltpu.SMEM),
             pl.BlockSpec(memory_space=pltpu.SMEM),

time: 19.8 us -> 18 us (0.909)
  Pallas kernels: 17.5 us -> 16.5 us
  local copies, waits for them, and re-layouts: 1.57 us -> 0.66 us
    pallas_call x1, Pallas kernels: 17.5 us -> 16.5 us  [shards(): pl.pallas_call(functools.partial(kernel, (fields, rows, width, cap, bands...]
    unnamed x1, local copies, waits for them, and re-layouts: 1.57 us -> 0.66 us
where the time goes in v3:
time: 18 us; the launch traced here: 17.8 us
  Pallas kernels  16.5 us (92%)
  local copies, waits for them, and re-layouts  0.66 us (4%)
  between operations  0.66 us (4%)
    pallas_call x1, Pallas kernels, shards(): pl.pallas_call(functools.partial(kernel, (fields, rows, width, cap, bands...  16.5 us
    unnamed x1, local copies, waits for them, and re-layouts  0.66 us

profile of v3, /device:TPU:0, one launch (start us, length us, event | category | flops | bytes accessed | tf_op | source)
XLA Modules:
  0.0 17.8 jit_solution(14015508733054972915)
XLA Ops:
  0.7 16.5 %shard_map.55 = f32[32,1024]{1,0:T(8,128)S(1)} custom-call(s32[32]{0:T(128)} %bitcast.6, s32[32]{0:T(128)} %bitcast.7, s32[1,1]{1,0:T(1,128)S(6)} %copy.8.live_ref, bf16[256,128]{1,0:T(8,128)(2,1)} %bitcast.5, bf16[32,384,128]{2,1,0:T(8,128)(2,1)} %bitcast.4), custom_call_target="tpu_custom_call" | custom-call | tf_op jit(solution)/shard_map/pallas_call | solution.py:184
  17.2 0.7 %copy.7 = f32[32,1024]{1,0:T(8,128)} copy(f32[32,1024]{1,0:T(8,128)S(1)} %shard_map.55) | data formatting | bytes 262144

commit v4 on v3

--- a/solution.py
+++ b/solution.py
@@ -12,8 +12,8 @@
 
 
 def kernel(
-    sizes, row_ref, code_ref, live_ref, flux_ref, weight_ref, out_ref,
-    table, found, xin, x32, op, wv, prefix, halo_out, halo_in, a_out, a_in, b_out, b_in,
+    sizes, row_hbm, code_hbm, live_ref, flux_ref, weight_ref, out_ref,
+    row_ref, code_ref, table, found, xin, x32, op, wv, prefix, halo_out, halo_in, a_out, a_in, b_out, b_in,
     in_sem, halo_send, halo_recv, a_send, a_recv, b_send, b_recv,
 ):
     fields, rows, width, cap, bands, subs = sizes
@@ -23,8 +23,19 @@
     y, core = s // 2, s % 2
     up, down = (b + 1) % bands, (b + bands - 1) % bands
 
+    barrier = pltpu.get_barrier_semaphore()
+    for other in range(1, subs):
+        pl.semaphore_signal(barrier, inc=1, device_id=(b, (s + other) % subs), device_id_type=MESH)
+    for other in range(ny):
+        pl.semaphore_signal(barrier, inc=1, device_id=(up, other * 2 + core), device_id_type=MESH)
+        pl.semaphore_signal(barrier, inc=1, device_id=(down, other * 2 + core), device_id_type=MESH)
+
     copy_flux = pltpu.make_async_copy(flux_ref, xin, in_sem.at[0])
     copy_flux.start()
+    small = []
+    for k, (source, place) in enumerate(((code_hbm, code_ref), (row_hbm, row_ref))):
+        small.append(pltpu.make_async_copy(source, place, in_sem.at[5 + k]))
+        small[-1].start()
     copy_w0 = pltpu.make_async_copy(weight_ref.at[:, :width], wv.at[:, :width], in_sem.at[1])
     copy_w0.start()
     half = cap // 2
@@ -34,13 +45,42 @@
         copy_w.append(pltpu.make_async_copy(weight_ref.at[where], wv.at[where], in_sem.at[2 + part]))
         copy_w[-1].start()
 
-    barrier = pltpu.get_barrier_semaphore()
-    for other in range(1, subs):
-        pl.semaphore_signal(barrier, inc=1, device_id=(b, (s + other) % subs), device_id_type=MESH)
-    for other in range(ny):
-        pl.semaphore_signal(barrier, inc=1, device_id=(up, other * 2 + core), device_id_type=MESH)
-        pl.semaphore_signal(barrier, inc=1, device_id=(down, other * 2 + core), device_id_type=MESH)
-
+    copy_flux.wait()
+    x32[...] = xin[...].astype(jnp.float32)
+    lane = lax.broadcasted_iota(jnp.int32, (fields, width), 1)
+
+    def row(i):
+        return x32[pl.ds(i, fields, stride=rows), :]
+
+    first = jnp.zeros((fields, width), jnp.float32)
+    last = jnp.zeros((fields, width), jnp.float32)
+    for i in range(rows):
+        x = row(i)
+        first = jnp.where(lane == i, x[:, :1], first)
+        last = jnp.where(lane == i, x[:, width - 1:], last)
+    halo_out[0] = row(rows - 1).astype(jnp.bfloat16)
+    halo_out[1] = row(0).astype(jnp.bfloat16)
+    halo_out[2] = last.astype(jnp.bfloat16)
+    halo_out[3] = first.astype(jnp.bfloat16)
+
+    pl.semaphore_wait(barrier, subs - 1 + 2 * ny)
+
+    partners = ((up, s), (down, s), (b, (s + 1) % subs), (b, (s + subs - 1) % subs))
+    sends = (b < bands - 1, b > 0, s < subs - 1, s > 0)
+    receives = (b > 0, b < bands - 1, s > 0, s < subs - 1)
+    halos = [
+        pltpu.make_async_remote_copy(
+            src_ref=halo_out.at[k], dst_ref=halo_in.at[k], send_sem=halo_send.at[k], recv_sem=halo_recv.at[k],
+            device_id=partners[k], device_id_type=MESH)
+        for k in range(4)
+    ]
+    for k in range(4):
+        @pl.when(sends[k])
+        def _(k=k):
+            halos[k].start()
+
+    for copy in small:
+        copy.wait()
     part_row = lax.broadcasted_iota(jnp.int32, table.shape, 0)
     part_lane = lax.broadcasted_iota(jnp.int32, table.shape, 1)
     wanted = jnp.where(part_lane < 2 * OB_DEV, (part_row - 1) * 2 * OB_DEV + part_lane, -1)
@@ -54,42 +94,9 @@
     copy_found = pltpu.make_async_copy(table, found, in_sem.at[4])
     copy_found.start()
 
-    copy_flux.wait()
-    x32[...] = xin[...].astype(jnp.float32)
-    lane = lax.broadcasted_iota(jnp.int32, (fields, width), 1)
-
-    def row(i):
-        return x32[pl.ds(i, fields, stride=rows), :]
-
-    first = jnp.zeros((fields, width), jnp.float32)
-    last = jnp.zeros((fields, width), jnp.float32)
     for i in range(rows):
-        x = row(i)
-        op[i, :, :width] = x.astype(jnp.bfloat16)
-        first = jnp.where(lane == i, x[:, :1], first)
-        last = jnp.where(lane == i, x[:, width - 1:], last)
-    halo_out[0] = row(rows - 1).astype(jnp.bfloat16)
-    halo_out[1] = row(0).astype(jnp.bfloat16)
-    halo_out[2] = last.astype(jnp.bfloat16)
-    halo_out[3] = first.astype(jnp.bfloat16)
+        op[i, :, :width] = row(i).astype(jnp.bfloat16)
     prefix[cap] = jnp.zeros((fields, width), jnp.float32)
-
-    pl.semaphore_wait(barrier, subs - 1 + 2 * ny)
-
-    partners = ((up, s), (down, s), (b, (s + 1) % subs), (b, (s + subs - 1) % subs))
-    sends = (b < bands - 1, b > 0, s < subs - 1, s > 0)
-    receives = (b > 0, b < bands - 1, s > 0, s < subs - 1)
-    halos = [
-        pltpu.make_async_remote_copy(
-            src_ref=halo_out.at[k], dst_ref=halo_in.at[k], send_sem=halo_send.at[k], recv_sem=halo_recv.at[k],
-            device_id=partners[k], device_id_type=MESH)
-        for k in range(4)
-    ]
-    for k in range(4):
-        @pl.when(sends[k])
-        def _(k=k):
-            halos[k].start()
-
     copy_w0.wait()
 
     def flux_part(e, carry):
@@ -185,14 +192,16 @@
         functools.partial(kernel, (fields, rows, width, cap, bands, subs)),
         out_shape=pltpu.VMEM((fields, OB_DEV * width), jnp.float32),
         in_specs=[
-            pl.BlockSpec(memory_space=pltpu.SMEM),
-            pl.BlockSpec(memory_space=pltpu.SMEM),
+            pl.BlockSpec(memory_space=pltpu.HBM),
+            pl.BlockSpec(memory_space=pltpu.HBM),
             pl.BlockSpec(memory_space=pltpu.SMEM),
             pl.BlockSpec(memory_space=pltpu.HBM),
             pl.BlockSpec(memory_space=pltpu.HBM),
         ],
         out_specs=pl.BlockSpec(memory_space=pltpu.VMEM),
         scratch_shapes=[
+            pltpu.SMEM((cap,), jnp.int32),
+            pltpu.SMEM((cap,), jnp.int32),
             pltpu.VMEM(table, jnp.int32),
             pltpu.SMEM(table, jnp.int32),
             pltpu.VMEM((fields * rows, width), jnp.bfloat16),
@@ -206,7 +215,7 @@
             pltpu.VMEM((pieces,) + block, jnp.bfloat16),
             pltpu.VMEM((pieces - 1,) + block, jnp.bfloat16),
             pltpu.VMEM((pieces - 1,) + block, jnp.bfloat16),
-            pltpu.SemaphoreType.DMA((5,)),
+            pltpu.SemaphoreType.DMA((7,)),
             pltpu.SemaphoreType.DMA((4,)),
             pltpu.SemaphoreType.DMA((4,)),
             pltpu.SemaphoreType.DMA((pieces,)),

time: 18 us -> 17.5 us (0.972)
  Pallas kernels: 16.5 us -> 16 us
    pallas_call x1, Pallas kernels: 16.5 us -> 16 us  [shards(): pl.pallas_call(functools.partial(kernel, (fields, rows, width, cap, bands...]
where the time goes in v4:
time: 17.5 us; the launch traced here: 17.3 us
  Pallas kernels  16 us (91%)
  local copies, waits for them, and re-layouts  0.66 us (4%)
  between operations  0.66 us (4%)
    pallas_call x1, Pallas kernels, shards(): pl.pallas_call(functools.partial(kernel, (fields, rows, width, cap, bands...  16 us
    unnamed x1, local copies, waits for them, and re-layouts  0.66 us

profile of v4, /device:TPU:0, one launch (start us, length us, event | category | flops | bytes accessed | tf_op | source)
XLA Modules:
  0.0 17.3 jit_solution(9340107423334147455)
XLA Ops:
  0.7 16.0 %shard_map.55 = f32[32,1024]{1,0:T(8,128)S(1)} custom-call(s32[32]{0:T(128)} %bitcast.6, s32[32]{0:T(128)} %bitcast.7, s32[1,1]{1,0:T(1,128)S(6)} %copy.8.live_ref, bf16[256,128]{1,0:T(8,128)(2,1)} %bitcast.5, bf16[32,384,128]{2,1,0:T(8,128)(2,1)} %bitcast.4), custom_call_target="tpu_custom_call" | custom-call | tf_op jit(solution)/shard_map/pallas_call | solution.py:191
  16.7 0.7 %copy.7 = f32[32,1024]{1,0:T(8,128)} copy(f32[32,1024]{1,0:T(8,128)S(1)} %shard_map.55) | data formatting | bytes 262144

commit v5 on v4

--- a/solution.py
+++ b/solution.py
@@ -104,7 +104,7 @@
         prefix[e] = jnp.dot(picked, wv[e, :width], preferred_element_type=jnp.float32)
         return carry
 
-    lax.fori_loop(0, cap, flux_part, 0, unroll=True)
+    lax.fori_loop(0, cap, flux_part, 0, unroll=8)
 
     for k in range(4):
         @pl.when(receives[k])
@@ -137,16 +137,18 @@
 
     for part in range(2):
         copy_w[part].wait()
-        lax.fori_loop(part * half, (part + 1) * half, gradient_part, 0, unroll=True)
+    lax.fori_loop(0, cap, gradient_part, 0, unroll=16)
     copy_found.wait()
-    lax.fori_loop(0, cap, chain, 0, unroll=True)
+    lax.fori_loop(0, cap, chain, 0, unroll=8)
 
     def partial(sub, step, q):
         return prefix[found[1 + sub, step * OB_DEV + q]]
 
     pieces = [(j, 1) for j in range(1, ny)] + [(0, 1)] + [(j, 0) for j in range(1, ny)] + [(0, 0)]
     swaps, moves = [], []
-    for p, (j, step) in enumerate(pieces):
+
+    def swap(p):
+        j, step = pieces[p]
         target = (y + j) % ny * 2 + 1 - core
         for q in range(OB_DEV):
             a_out[p, q] = partial(target, step, q).astype(jnp.bfloat16)
@@ -154,21 +156,31 @@
             src_ref=a_out.at[p], dst_ref=a_in.at[p], send_sem=a_send.at[p], recv_sem=a_recv.at[p],
             device_id=(b, y * 2 + 1 - core), device_id_type=MESH))
         swaps[-1].start()
-    for p, (j, step) in enumerate(pieces):
+
+    def move(p):
+        j, step = pieces[p]
         target = (y + j) % ny * 2 + core
         swaps[p].wait_recv()
         if (j, step) == (0, 0):
             for q in range(OB_DEV):
                 out_ref[:, q * width:(q + 1) * width] = partial(target, step, q) + a_in[p, q].astype(jnp.float32)
-            continue
+            return
         for q in range(OB_DEV):
             b_out[p, q] = (partial(target, step, q) + a_in[p, q].astype(jnp.float32)).astype(jnp.bfloat16)
         moves.append(pltpu.make_async_remote_copy(
             src_ref=b_out.at[p], dst_ref=b_in.at[p], send_sem=b_send.at[p], recv_sem=b_recv.at[p],
             device_id=(up if step else b, target), device_id_type=MESH))
         moves[-1].start()
-    for p, move in enumerate(moves):
-        move.wait_recv()
+
+    ahead = ny
+    for p in range(ahead):
+        swap(p)
+    for p in range(len(pieces)):
+        move(p)
+        if p + ahead < len(pieces):
+            swap(p + ahead)
+    for p, arrival in enumerate(moves):
+        arrival.wait_recv()
         for q in range(OB_DEV):
             out_ref[:, q * width:(q + 1) * width] += b_in[p, q].astype(jnp.float32)
 

time: 17.5 us -> 17.5 us (level)
  no operation moved by 1% of the time
where the time goes in v5:
time: 17.5 us; the launch traced here: 17.3 us
  Pallas kernels  16 us (91%)
  local copies, waits for them, and re-layouts  0.66 us (4%)
  between operations  0.66 us (4%)
    pallas_call x1, Pallas kernels, shards(): pl.pallas_call(functools.partial(kernel, (fields, rows, width, cap, bands...  16 us
    unnamed x1, local copies, waits for them, and re-layouts  0.66 us

profile of v5, /device:TPU:0, one launch (start us, length us, event | category | flops | bytes accessed | tf_op | source)
XLA Modules:
  0.0 17.3 jit_solution(12222761891627299846)
XLA Ops:
  0.7 16.0 %shard_map.55 = f32[32,1024]{1,0:T(8,128)S(1)} custom-call(s32[32]{0:T(128)} %bitcast.6, s32[32]{0:T(128)} %bitcast.7, s32[1,1]{1,0:T(1,128)S(6)} %copy.8.live_ref, bf16[256,128]{1,0:T(8,128)(2,1)} %bitcast.5, bf16[32,384,128]{2,1,0:T(8,128)(2,1)} %bitcast.4), custom_call_target="tpu_custom_call" | custom-call | tf_op jit(solution)/shard_map/pallas_call | solution.py:203
  16.7 0.7 %copy.7 = f32[32,1024]{1,0:T(8,128)} copy(f32[32,1024]{1,0:T(8,128)S(1)} %shard_map.55) | data formatting | bytes 262144

commit v6 on v5

--- a/solution.py
+++ b/solution.py
@@ -13,7 +13,7 @@
 
 def kernel(
     sizes, row_hbm, code_hbm, live_ref, flux_ref, weight_ref, out_ref,
-    row_ref, code_ref, table, found, xin, x32, op, wv, prefix, halo_out, halo_in, a_out, a_in, b_out, b_in,
+    row_ref, code_ref, table, found, xin, x32, dx, op, wv, prefix, halo_out, halo_in, a_out, a_in, b_out, b_in,
     in_sem, halo_send, halo_recv, a_send, a_recv, b_send, b_recv,
 ):
     fields, rows, width, cap, bands, subs = sizes
@@ -95,7 +95,13 @@
     copy_found.start()
 
     for i in range(rows):
-        op[i, :, :width] = row(i).astype(jnp.bfloat16)
+        x = row(i)
+        op[i, :, :width] = x.astype(jnp.bfloat16)
+        east = jnp.where(lane == width - 1, 0.0, pltpu.roll(x, width - 1, 1))
+        west = jnp.where(lane == 0, 0.0, pltpu.roll(x, 1, 1))
+        dx[i] = east - west
+        if 0 < i < rows - 1:
+            op[i, :, 2 * width:] = (0.5 * (row(i + 1) - row(i - 1))).astype(jnp.bfloat16)
     prefix[cap] = jnp.zeros((fields, width), jnp.float32)
     copy_w0.wait()
 
@@ -117,13 +123,10 @@
 
     below, above, left, right = (halo_in[k].astype(jnp.float32) for k in range(4))
     for i in range(rows):
-        x = row(i)
-        before = row(i - 1) if i > 0 else below
-        after = row(i + 1) if i < rows - 1 else above
-        west = jnp.where(lane == 0, left[:, i:i + 1], pltpu.roll(x, 1, 1))
-        east = jnp.where(lane == width - 1, right[:, i:i + 1], pltpu.roll(x, width - 1, 1))
-        op[i, :, width:2 * width] = (0.5 * (east - west)).astype(jnp.bfloat16)
-        op[i, :, 2 * width:] = (0.5 * (after - before)).astype(jnp.bfloat16)
+        edge = jnp.where(lane == 0, -left[:, i:i + 1], jnp.where(lane == width - 1, right[:, i:i + 1], 0.0))
+        op[i, :, width:2 * width] = (0.5 * (dx[i] + edge)).astype(jnp.bfloat16)
+    op[0, :, 2 * width:] = (0.5 * (row(1) - below)).astype(jnp.bfloat16)
+    op[rows - 1, :, 2 * width:] = (0.5 * (above - row(rows - 2))).astype(jnp.bfloat16)
 
     def gradient_part(e, carry):
         picked = op[row_ref[e], :, width:]
@@ -144,35 +147,39 @@
     def partial(sub, step, q):
         return prefix[found[1 + sub, step * OB_DEV + q]]
 
-    pieces = [(j, 1) for j in range(1, ny)] + [(0, 1)] + [(j, 0) for j in range(1, ny)] + [(0, 0)]
+    away = [(j, 1) for j in range(1, ny)] + [(0, 1)] + [(j, 0) for j in range(1, ny)] + [(0, 0)]
+    count = a_out.shape[1]
+    cuts = OB_DEV // count
+    pieces = [(j, step, cut * count) for j, step in away for cut in range(cuts)]
     swaps, moves = [], []
 
     def swap(p):
-        j, step = pieces[p]
+        j, step, lead = pieces[p]
         target = (y + j) % ny * 2 + 1 - core
-        for q in range(OB_DEV):
-            a_out[p, q] = partial(target, step, q).astype(jnp.bfloat16)
+        for q in range(count):
+            a_out[p, q] = partial(target, step, lead + q).astype(jnp.bfloat16)
         swaps.append(pltpu.make_async_remote_copy(
             src_ref=a_out.at[p], dst_ref=a_in.at[p], send_sem=a_send.at[p], recv_sem=a_recv.at[p],
             device_id=(b, y * 2 + 1 - core), device_id_type=MESH))
         swaps[-1].start()
 
     def move(p):
-        j, step = pieces[p]
+        j, step, lead = pieces[p]
         target = (y + j) % ny * 2 + core
         swaps[p].wait_recv()
         if (j, step) == (0, 0):
-            for q in range(OB_DEV):
-                out_ref[:, q * width:(q + 1) * width] = partial(target, step, q) + a_in[p, q].astype(jnp.float32)
+            for q in range(count):
+                columns = slice((lead + q) * width, (lead + q + 1) * width)
+                out_ref[:, columns] = partial(target, step, lead + q) + a_in[p, q].astype(jnp.float32)
             return
-        for q in range(OB_DEV):
-            b_out[p, q] = (partial(target, step, q) + a_in[p, q].astype(jnp.float32)).astype(jnp.bfloat16)
+        for q in range(count):
+            b_out[p, q] = (partial(target, step, lead + q) + a_in[p, q].astype(jnp.float32)).astype(jnp.bfloat16)
         moves.append(pltpu.make_async_remote_copy(
             src_ref=b_out.at[p], dst_ref=b_in.at[p], send_sem=b_send.at[p], recv_sem=b_recv.at[p],
             device_id=(up if step else b, target), device_id_type=MESH))
         moves[-1].start()
 
-    ahead = ny
+    ahead = ny * cuts
     for p in range(ahead):
         swap(p)
     for p in range(len(pieces)):
@@ -181,8 +188,9 @@
             swap(p + ahead)
     for p, arrival in enumerate(moves):
         arrival.wait_recv()
-        for q in range(OB_DEV):
-            out_ref[:, q * width:(q + 1) * width] += b_in[p, q].astype(jnp.float32)
+        lead = pieces[p][2]
+        for q in range(count):
+            out_ref[:, (lead + q) * width:(lead + q + 1) * width] += b_in[p, q].astype(jnp.float32)
 
     for k in range(4):
         @pl.when(sends[k])
@@ -196,10 +204,11 @@
     fields, rows, width = atmos_flux.shape
     cap = weight_tiles.shape[2]
     bands, subs = lax.axis_size("band"), lax.axis_size("sub")
-    pieces = subs
+    cuts = 2
+    pieces = subs * cuts
 
     table = (-(-(1 + subs) // 8) * 8, 128)
-    block = (OB_DEV, fields, width)
+    block = (OB_DEV // cuts, fields, width)
     return pl.pallas_call(
         functools.partial(kernel, (fields, rows, width, cap, bands, subs)),
         out_shape=pltpu.VMEM((fields, OB_DEV * width), jnp.float32),
@@ -218,6 +227,7 @@
             pltpu.SMEM(table, jnp.int32),
             pltpu.VMEM((fields * rows, width), jnp.bfloat16),
             pltpu.VMEM((fields * rows, width), jnp.float32),
+            pltpu.VMEM((rows, fields, width), jnp.float32),
             pltpu.VMEM((rows, fields, 3 * width), jnp.bfloat16),
             pltpu.VMEM((cap, 3 * width, width), jnp.bfloat16),
             pltpu.VMEM((cap + 1, fields, width), jnp.float32),
@@ -225,15 +235,15 @@
             pltpu.VMEM((4, fields, width), jnp.bfloat16),
             pltpu.VMEM((pieces,) + block, jnp.bfloat16),
             pltpu.VMEM((pieces,) + block, jnp.bfloat16),
-            pltpu.VMEM((pieces - 1,) + block, jnp.bfloat16),
-            pltpu.VMEM((pieces - 1,) + block, jnp.bfloat16),
+            pltpu.VMEM((pieces - cuts,) + block, jnp.bfloat16),
+            pltpu.VMEM((pieces - cuts,) + block, jnp.bfloat16),
             pltpu.SemaphoreType.DMA((7,)),
             pltpu.SemaphoreType.DMA((4,)),
             pltpu.SemaphoreType.DMA((4,)),
             pltpu.SemaphoreType.DMA((pieces,)),
             pltpu.SemaphoreType.DMA((pieces,)),
-            pltpu.SemaphoreType.DMA((pieces - 1,)),
-            pltpu.SemaphoreType.DMA((pieces - 1,)),
+            pltpu.SemaphoreType.DMA((pieces - cuts,)),
+            pltpu.SemaphoreType.DMA((pieces - cuts,)),
         ],
         compiler_params=pltpu.CompilerParams(
             collective_id=0, has_side_effects=True, vmem_limit_bytes=60 * 1024 * 1024

time: 17.5 us -> 17.5 us (level)
  no operation moved by 1% of the time
where the time goes in v6:
time: 17.5 us; the launch traced here: 17.3 us
  Pallas kernels  16 us (91%)
  local copies, waits for them, and re-layouts  0.66 us (4%)
  between operations  0.66 us (4%)
    pallas_call x1, Pallas kernels, shards(): pl.pallas_call(functools.partial(kernel, (fields, rows, width, cap, bands...  16 us
    unnamed x1, local copies, waits for them, and re-layouts  0.66 us

profile of v6, /device:TPU:0, one launch (start us, length us, event | category | flops | bytes accessed | tf_op | source)
XLA Modules:
  0.0 17.3 jit_solution(13720851620058125753)
XLA Ops:
  0.7 16.0 %shard_map.55 = f32[32,1024]{1,0:T(8,128)S(1)} custom-call(s32[32]{0:T(128)} %bitcast.6, s32[32]{0:T(128)} %bitcast.7, s32[1,1]{1,0:T(1,128)S(6)} %copy.8.live_ref, bf16[256,128]{1,0:T(8,128)(2,1)} %bitcast.5, bf16[32,384,128]{2,1,0:T(8,128)(2,1)} %bitcast.4), custom_call_target="tpu_custom_call" | custom-call | tf_op jit(solution)/shard_map/pallas_call | solution.py:212
  16.7 0.7 %copy.7 = f32[32,1024]{1,0:T(8,128)} copy(f32[32,1024]{1,0:T(8,128)S(1)} %shard_map.55) | data formatting | bytes 262144

commit v7 on v6

--- a/solution.py
+++ b/solution.py
@@ -27,8 +27,11 @@
     for other in range(1, subs):
         pl.semaphore_signal(barrier, inc=1, device_id=(b, (s + other) % subs), device_id_type=MESH)
     for other in range(ny):
-        pl.semaphore_signal(barrier, inc=1, device_id=(up, other * 2 + core), device_id_type=MESH)
         pl.semaphore_signal(barrier, inc=1, device_id=(down, other * 2 + core), device_id_type=MESH)
+
+    @pl.when(b < bands - 1)
+    def _():
+        pl.semaphore_signal(barrier, inc=1, device_id=(up, s), device_id_type=MESH)
 
     copy_flux = pltpu.make_async_copy(flux_ref, xin, in_sem.at[0])
     copy_flux.start()
@@ -63,7 +66,7 @@
     halo_out[2] = last.astype(jnp.bfloat16)
     halo_out[3] = first.astype(jnp.bfloat16)
 
-    pl.semaphore_wait(barrier, subs - 1 + 2 * ny)
+    pl.semaphore_wait(barrier, subs - 1 + ny + jnp.where(b > 0, 1, 0))
 
     partners = ((up, s), (down, s), (b, (s + 1) % subs), (b, (s + subs - 1) % subs))
     sends = (b < bands - 1, b > 0, s < subs - 1, s > 0)

time: 17.5 us -> 17.4 us (level)
  no operation moved by 1% of the time
where the time goes in v7:
time: 17.4 us; the launch traced here: 17.3 us
  Pallas kernels  16 us (92%)
  local copies, waits for them, and re-layouts  0.66 us (4%)
  between operations  0.66 us (4%)
    pallas_call x1, Pallas kernels, shards(): pl.pallas_call(functools.partial(kernel, (fields, rows, width, cap, bands...  16 us
    unnamed x1, local copies, waits for them, and re-layouts  0.66 us

profile of v7, /device:TPU:0, one launch (start us, length us, event | category | flops | bytes accessed | tf_op | source)
XLA Modules:
  0.0 17.3 jit_solution(15527097737611297944)
XLA Ops:
  0.7 16.0 %shard_map.55 = f32[32,1024]{1,0:T(8,128)S(1)} custom-call(s32[32]{0:T(128)} %bitcast.6, s32[32]{0:T(128)} %bitcast.7, s32[1,1]{1,0:T(1,128)S(6)} %copy.8.live_ref, bf16[256,128]{1,0:T(8,128)(2,1)} %bitcast.5, bf16[32,384,128]{2,1,0:T(8,128)(2,1)} %bitcast.4), custom_call_target="tpu_custom_call" | custom-call | tf_op jit(solution)/shard_map/pallas_call | solution.py:215
  16.6 0.7 %copy.7 = f32[32,1024]{1,0:T(8,128)} copy(f32[32,1024]{1,0:T(8,128)S(1)} %shard_map.55) | data formatting | bytes 262144

commit v8 on v7

--- a/solution.py
+++ b/solution.py
@@ -143,9 +143,9 @@
 
     for part in range(2):
         copy_w[part].wait()
-    lax.fori_loop(0, cap, gradient_part, 0, unroll=16)
+    lax.fori_loop(0, cap, gradient_part, 0, unroll=True)
     copy_found.wait()
-    lax.fori_loop(0, cap, chain, 0, unroll=8)
+    lax.fori_loop(0, cap, chain, 0, unroll=True)
 
     def partial(sub, step, q):
         return prefix[found[1 + sub, step * OB_DEV + q]]
@@ -207,7 +207,7 @@
     fields, rows, width = atmos_flux.shape
     cap = weight_tiles.shape[2]
     bands, subs = lax.axis_size("band"), lax.axis_size("sub")
-    cuts = 2
+    cuts = 1
     pieces = subs * cuts
 
     table = (-(-(1 + subs) // 8) * 8, 128)

time: 17.4 us -> 17.2 us (0.989)
  Pallas kernels: 16 us -> 15.8 us
    pallas_call x1, Pallas kernels: 16 us -> 15.8 us  [shards(): pl.pallas_call(functools.partial(kernel, (fields, rows, width, cap, bands...]
where the time goes in v8:
time: 17.2 us; the launch traced here: 17.1 us
  Pallas kernels  15.8 us (92%)
  local copies, waits for them, and re-layouts  0.66 us (4%)
  between operations  0.66 us (4%)
    pallas_call x1, Pallas kernels, shards(): pl.pallas_call(functools.partial(kernel, (fields, rows, width, cap, bands...  15.8 us
    unnamed x1, local copies, waits for them, and re-layouts  0.66 us

profile of v8, /device:TPU:0, one launch (start us, length us, event | category | flops | bytes accessed | tf_op | source)
XLA Modules:
  0.0 17.1 jit_solution(14245722161123721950)
XLA Ops:
  0.7 15.8 %shard_map.55 = f32[32,1024]{1,0:T(8,128)S(1)} custom-call(s32[32]{0:T(128)} %bitcast.6, s32[32]{0:T(128)} %bitcast.7, s32[1,1]{1,0:T(1,128)S(6)} %copy.8.live_ref, bf16[256,128]{1,0:T(8,128)(2,1)} %bitcast.5, bf16[32,384,128]{2,1,0:T(8,128)(2,1)} %bitcast.4), custom_call_target="tpu_custom_call" | custom-call | tf_op jit(solution)/shard_map/pallas_call | solution.py:215
  16.4 0.7 %copy.7 = f32[32,1024]{1,0:T(8,128)} copy(f32[32,1024]{1,0:T(8,128)S(1)} %shard_map.55) | data formatting | bytes 262144
